TPU v7x, 32 devices: a whole 2x2x4 slice. The times are simulated.
32 devices in a mesh: seq: 8 (over y, x, core), tp: 4 (over z).
Axes of the slice: x: 2, y: 2, z: 4, core: 2. Of those that a mesh axis runs over, the one named last changes fastest.
Arguments:
- tokens: bfloat16 [1024, 4096], P('seq', 'tp'), may hold values from -6 to 6
- in_weight: bfloat16 [4096, 8192], P(None, 'tp'), may hold values from -0.09375 to 0.09375
- conv_weight: float32 [4, 8192], P(None, 'tp'), may hold values from -3 to 3
- conv_bias: float32 [8192], P('tp'), may hold values from -0.5 to 0.5
- proj_weight: bfloat16 [8192, 288], P('tp'), may hold values from -0.0625 to 0.0625
- dt_weight: bfloat16 [256, 8192], P(None, 'tp'), may hold values from -0.375 to 0.375
- dt_bias: float32 [8192], P('tp'), may hold values from -7 to -2
- a_log: float32 [16, 8192], P(None, 'tp'), may hold values from -3 to 1.5
- skip_gain: float32 [8192], P('tp'), may hold values from 0.5 to 1.5
- threshold: float32 [8192], P('tp'), may hold values from -0.5 to 0.5
Outputs:
- gated: bfloat16 [1024, 8192], P('seq', 'tp')
All inputs are finite; a program needn't handle non-finite values.
Results may differ from a plain program's by a relative error of at most 0.0085.
Values may be sent and summed in bfloat16 or wider, within the bound.
A program may use at most 64 MiB of HBM per device.

v0:
```python
import math

import jax
import jax.numpy as jnp
from jax import lax
from jax.sharding import PartitionSpec as P


def shifted(x, axis, by):
    peers = lax.axis_size(axis)
    pairs = [(i, i + by) for i in range(peers) if 0 <= i + by < peers]
    return lax.ppermute(x, axis, pairs)


def carried_in(value, axis, join, neutral):
    count, mine = (lax.axis_size(axis), lax.axis_index(axis))
    pieces = jax.tree.map(lambda part: lax.all_gather(part, axis), value)
    total = jax.tree.map(
        lambda part, zero: jnp.full_like(part, 0) + jnp.asarray(zero, part.dtype), value, neutral
    )

    def turn(position, total):
        longer = join(total, jax.tree.map(lambda part: part[position], pieces))
        return jax.tree.map(lambda new, old: jnp.where(position < mine, new, old), longer, total)

    return lax.fori_loop(0, count - 1, turn, total)


def combine_pair(earlier, later):
    return (earlier[0] * later[0], later[0] * earlier[1] + later[1])


def lower_table(rows):
    row_ids = lax.broadcasted_iota(jnp.int32, (rows, rows), 0)
    col_ids = lax.broadcasted_iota(jnp.int32, (rows, rows), 1)
    return row_ids >= col_ids


def local_pass(step_size, inflow_rows, b_coef, c_coef, rate, start_state, block):
    rows, width = step_size.shape
    count = rows // block
    lower = lower_table(block)
    lower_float = lower.astype(jnp.float32)

    def run(carry, items):
        state, decay_all = carry
        step_block, flow_block, b_block, c_block = items
        summed = jnp.dot(
            lower_float,
            step_block,
            precision=lax.Precision.HIGHEST,
            preferred_element_type=jnp.float32,
        )
        diff = jnp.where(lower[:, :, None], summed[:, None, :] - summed[None, :, :], 0.0)
        weights = jnp.where(
            lower[:, :, None, None], jnp.exp(diff[:, :, None, :] * rate[None, None]), 0.0
        )
        inflow = flow_block[:, None, :] * b_block[:, :, None]
        states = jnp.einsum("tsnc,snc->tnc", weights, inflow, precision=lax.Precision.HIGHEST)
        states = states + jnp.exp(summed[:, None, :] * rate[None]) * state[None]
        outputs = jnp.einsum("tn,tnc->tc", c_block, states, precision=lax.Precision.HIGHEST)
        block_decay = jnp.exp(summed[-1][None, :] * rate)
        return ((states[-1], block_decay * decay_all), outputs)

    items = (
        step_size.reshape(count, block, width),
        inflow_rows.reshape(count, block, width),
        b_coef.reshape(count, block, -1),
        c_coef.reshape(count, block, -1),
    )
    (end_state, decay_all), outputs = lax.scan(
        run, (start_state, jnp.ones_like(start_state)), items
    )
    return (end_state, decay_all, outputs.reshape(rows, width))


def per_device(
    tokens,
    in_weight,
    conv_weight,
    conv_bias,
    proj_weight,
    dt_weight,
    dt_bias,
    a_log,
    skip_gain,
    threshold,
):
    tok_rows = tokens.shape[0]
    width = in_weight.shape[1]
    taps = conv_weight.shape[0]
    rank = dt_weight.shape[0]
    states_n = a_log.shape[0]
    projected = jnp.dot(
        lax.all_gather(tokens, "tp", axis=1, tiled=True),
        in_weight,
        preferred_element_type=jnp.float32,
    ).astype(jnp.bfloat16)
    rim_inner = shifted(projected[tok_rows - taps + 1 :], "seq", 1)
    padded = jnp.concatenate([rim_inner, projected], axis=0)
    pre = conv_bias[None, :] + jnp.zeros((tok_rows, width), jnp.float32)
    for k in range(taps):
        pre = pre + conv_weight[k][None, :] * padded[k : k + tok_rows].astype(jnp.float32)
    u_half = jax.nn.silu(pre).astype(jnp.bfloat16)
    partial_sums = jnp.dot(u_half, proj_weight, preferred_element_type=jnp.float32)
    total = lax.psum(partial_sums, "tp")
    dt_low = total[:, :rank].astype(jnp.bfloat16)
    b_coef = total[:, rank : rank + states_n]
    c_coef = total[:, rank + states_n :]
    step_size = jax.nn.softplus(
        jnp.dot(dt_low, dt_weight, preferred_element_type=jnp.float32) + dt_bias[None, :]
    )
    rate = -jnp.exp(a_log)
    u_float = u_half.astype(jnp.float32)
    inflow_rows = step_size * u_float
    block = math.gcd(tok_rows, 16)
    zero_state = jnp.zeros((states_n, width), jnp.float32)
    end_state, decay_all, local_out = local_pass(
        step_size, inflow_rows, b_coef, c_coef, rate, zero_state, block
    )
    incoming = carried_in(
        (decay_all, end_state), "seq", combine_pair, (jnp.ones_like(decay_all), zero_state)
    )
    entry_state = incoming[1]
    whole_lower = lower_table(tok_rows).astype(jnp.float32)
    summed = jnp.dot(
        whole_lower, step_size, precision=lax.Precision.HIGHEST, preferred_element_type=jnp.float32
    )
    growth = jnp.exp(summed[:, None, :] * rate[None])
    scan_out = local_out + jnp.einsum(
        "tn,tnc->tc", c_coef, growth * entry_state[None], precision=lax.Precision.HIGHEST
    )
    y_full = scan_out + skip_gain[None, :] * u_float
    return (y_full * jax.nn.sigmoid(4.0 * (y_full - threshold[None, :]))).astype(jnp.bfloat16)


def solution(mesh):
    return jax.shard_map(
        per_device,
        mesh=mesh,
        in_specs=(
            P("seq", "tp"),
            P(None, "tp"),
            P(None, "tp"),
            P("tp"),
            P("tp", None),
            P(None, "tp"),
            P("tp"),
            P(None, "tp"),
            P("tp"),
            P("tp"),
        ),
        out_specs=P("seq", "tp"),
        check_vma=False,
    )
```

profile of v0, /device:TPU:5, one launch (start us, length us, event | category | flops | bytes accessed | tf_op | source)
XLA Modules:
  0.0 270.8 jit_solution(18380266906771726925)
XLA Ops:
  6.5 0.7 all-gather.6.cloned.1.call-update
  7.3 30.6 %all-gather.6.cloned.1.call-done = bf16[128,4096]{1,0:T(8,128)(2,1)} async-done(((bf16[128,1024]{1,0:T(8,128)(2,1)}), bf16[128,4096]{1,0:T(8,128)(2,1)}) %all-gather.6.cloned.1.call-update) | async-done | bytes 1048592 | tf_op jit(solution)/shard_map/all_gather | solution.py:95
  38.0 8.4 %convolution_convert_fusion = bf16[128,2048]{1,0:T(8,128)(2,1)S(1)} fusion(bf16[128,4096]{1,0:T(8,128)(2,1)} %all-gather.6.cloned.1.call-done, bf16[4096,2048]{1,0:T(8,128)(2,1)} %param.15), kind=kOutput, calls=%fused_computation.30 | convolution fusion | flops 2147745792 | bytes 18350080 | tf_op jit(solution)/shard_map/dot_general | solution.py:94
  46.5 3.9 %collective-permute-start = (bf16[3,2048]{1,0:T(4,128)(2,1)S(1)}, bf16[3,2048]{1,0:T(4,128)(2,1)S(1)}, u32[]{:S(2)}, u32[]{:S(2)}) collective-permute-start(bf16[3,2048]{1,0:T(4,128)(2,1)S(1)} %slice.57), channel_id=1, source_target_pairs={{0,4},{4,8},{8,12},{12,16},{16,20},{20,24},{24,28},{1,5},{5,9},{9,... | collective-permute-start | bytes 36872 | tf_op jit(solution)/shard_map/ppermute | solution.py:12
  50.4 0.8 collective-permute-done
  51.2 0.7 multiply_convert_fusion.1
  52.0 1.1 fusion.23
  53.3 32.5 %all-reduce.2.cloned.1.call-done = f32[128,288]{0,1:T(8,128)} async-done(((f32[128,288]{0,1:T(8,128)}), f32[128,288]{0,1:T(8,128)}) %all-reduce.2.cloned.1.call-update) | async-done | bytes 147472 | tf_op jit(solution)/shard_map/psum | solution.py:106
  85.8 0.7 fusion.20
  86.7 3.2 %convert_multiply_fusion.1 = (f32[128,2048]{1,0:T(8,128)}, f32[128,2048]{1,0:T(8,128)S(1)}) fusion(bf16[128,2048]{1,0:T(8,128)(2,1)S(1)} %multiply_convert_fusion.1, f32[2048]{0:T(1024)S(1)} %copy-done.7, bf16[256,2048]{1,0:T(8,128)(2,1)} %param.19, f32[128,288]{0,1:T(8,128)} %all-reduce.2.cloned.1.call-done), kind=kOutput, calls=%fused_computation.32 | convolution fusion | flops 136577024 | bytes 3743744 | tf_op jit(solution)/shard_map/dot_general | solution.py:111
  89.9 100.8 %while.31 = (s32[]{:T(128)}, f32[16,2048]{1,0:T(8,128)S(1)}, f32[16,2048]{1,0:T(8,128)S(1)}, f32[8,16,2048]{2,1,0:T(8,128)}, f32[8,16,2048]{2,1,0:T(8,128)}, /*i...) while((s32[]{:T(128)}, f32[16,2048]{1,0:T(8,128)S(1)}, ...), condition=%wide.region_2.3_spmd.clone.clone, body=%wide.region_1.2_spmd.clone.clone.sunk | while | flops 48857856 | bytes 19168648 | solution.py:71
  90.2 0.9 dynamic-slice_bitcast_fusion.5
  91.5 8.7 %multiply_reduce_fusion.2 = f32[16,2048,16]{1,0,2:T(8,128)S(1)} fusion(f32[16,2048,16]{1,0,2:T(8,128)S(1)} %get-tuple-element.379, f32[16,2048]{1,0:T(8,128)S(1)} %get-tuple-element.410, f32[16,16,2048]{2,1,0:T(8,128)S(1)} %get-tuple-element.380, pred[16,16]{1,0:T(8,128)(4,1)S(1)} %iota_compare_fusion.5), kind=kLoop, calls=%fused_computation.5.clone.1 | loop fusion | flops 33030144 | bytes 6422784 | tf_op jit(solution)/shard_map/while/body/eval_jaxpr/tsnc,snc->tnc/dot_general | solution.py:59
  100.6 1.1 fusion.44
  102.8 0.9 dynamic-slice_bitcast_fusion.5
  104.1 8.7 %multiply_reduce_fusion.2 = f32[16,2048,16]{1,0,2:T(8,128)S(1)} fusion(f32[16,2048,16]{1,0,2:T(8,128)S(1)} %get-tuple-element.379, f32[16,2048]{1,0:T(8,128)S(1)} %get-tuple-element.410, f32[16,16,2048]{2,1,0:T(8,128)S(1)} %get-tuple-element.380, pred[16,16]{1,0:T(8,128)(4,1)S(1)} %iota_compare_fusion.5), kind=kLoop, calls=%fused_computation.5.clone.1 | loop fusion | flops 33030144 | bytes 6422784 | tf_op jit(solution)/shard_map/while/body/eval_jaxpr/tsnc,snc->tnc/dot_general | solution.py:59
  113.2 1.1 fusion.44
  115.4 0.9 dynamic-slice_bitcast_fusion.5
  116.7 8.7 %multiply_reduce_fusion.2 = f32[16,2048,16]{1,0,2:T(8,128)S(1)} fusion(f32[16,2048,16]{1,0,2:T(8,128)S(1)} %get-tuple-element.379, f32[16,2048]{1,0:T(8,128)S(1)} %get-tuple-element.410, f32[16,16,2048]{2,1,0:T(8,128)S(1)} %get-tuple-element.380, pred[16,16]{1,0:T(8,128)(4,1)S(1)} %iota_compare_fusion.5), kind=kLoop, calls=%fused_computation.5.clone.1 | loop fusion | flops 33030144 | bytes 6422784 | tf_op jit(solution)/shard_map/while/body/eval_jaxpr/tsnc,snc->tnc/dot_general | solution.py:59
  125.8 1.1 fusion.44
  128.0 0.9 dynamic-slice_bitcast_fusion.5
  129.3 8.7 %multiply_reduce_fusion.2 = f32[16,2048,16]{1,0,2:T(8,128)S(1)} fusion(f32[16,2048,16]{1,0,2:T(8,128)S(1)} %get-tuple-element.379, f32[16,2048]{1,0:T(8,128)S(1)} %get-tuple-element.410, f32[16,16,2048]{2,1,0:T(8,128)S(1)} %get-tuple-element.380, pred[16,16]{1,0:T(8,128)(4,1)S(1)} %iota_compare_fusion.5), kind=kLoop, calls=%fused_computation.5.clone.1 | loop fusion | flops 33030144 | bytes 6422784 | tf_op jit(solution)/shard_map/while/body/eval_jaxpr/tsnc,snc->tnc/dot_general | solution.py:59
  138.4 1.1 fusion.44
  140.6 0.9 dynamic-slice_bitcast_fusion.5
  141.9 8.7 %multiply_reduce_fusion.2 = f32[16,2048,16]{1,0,2:T(8,128)S(1)} fusion(f32[16,2048,16]{1,0,2:T(8,128)S(1)} %get-tuple-element.379, f32[16,2048]{1,0:T(8,128)S(1)} %get-tuple-element.410, f32[16,16,2048]{2,1,0:T(8,128)S(1)} %get-tuple-element.380, pred[16,16]{1,0:T(8,128)(4,1)S(1)} %iota_compare_fusion.5), kind=kLoop, calls=%fused_computation.5.clone.1 | loop fusion | flops 33030144 | bytes 6422784 | tf_op jit(solution)/shard_map/while/body/eval_jaxpr/tsnc,snc->tnc/dot_general | solution.py:59
  151.0 1.1 fusion.44
  153.2 0.9 dynamic-slice_bitcast_fusion.5
  154.5 8.7 %multiply_reduce_fusion.2 = f32[16,2048,16]{1,0,2:T(8,128)S(1)} fusion(f32[16,2048,16]{1,0,2:T(8,128)S(1)} %get-tuple-element.379, f32[16,2048]{1,0:T(8,128)S(1)} %get-tuple-element.410, f32[16,16,2048]{2,1,0:T(8,128)S(1)} %get-tuple-element.380, pred[16,16]{1,0:T(8,128)(4,1)S(1)} %iota_compare_fusion.5), kind=kLoop, calls=%fused_computation.5.clone.1 | loop fusion | flops 33030144 | bytes 6422784 | tf_op jit(solution)/shard_map/while/body/eval_jaxpr/tsnc,snc->tnc/dot_general | solution.py:59
  163.6 1.1 fusion.44
  165.8 0.9 dynamic-slice_bitcast_fusion.5
  167.1 8.7 %multiply_reduce_fusion.2 = f32[16,2048,16]{1,0,2:T(8,128)S(1)} fusion(f32[16,2048,16]{1,0,2:T(8,128)S(1)} %get-tuple-element.379, f32[16,2048]{1,0:T(8,128)S(1)} %get-tuple-element.410, f32[16,16,2048]{2,1,0:T(8,128)S(1)} %get-tuple-element.380, pred[16,16]{1,0:T(8,128)(4,1)S(1)} %iota_compare_fusion.5), kind=kLoop, calls=%fused_computation.5.clone.1 | loop fusion | flops 33030144 | bytes 6422784 | tf_op jit(solution)/shard_map/while/body/eval_jaxpr/tsnc,snc->tnc/dot_general | solution.py:59
  176.2 1.1 fusion.44
  178.4 0.9 dynamic-slice_bitcast_fusion.5
  179.7 8.7 %multiply_reduce_fusion.2 = f32[16,2048,16]{1,0,2:T(8,128)S(1)} fusion(f32[16,2048,16]{1,0,2:T(8,128)S(1)} %get-tuple-element.379, f32[16,2048]{1,0:T(8,128)S(1)} %get-tuple-element.410, f32[16,16,2048]{2,1,0:T(8,128)S(1)} %get-tuple-element.380, pred[16,16]{1,0:T(8,128)(4,1)S(1)} %iota_compare_fusion.5), kind=kLoop, calls=%fused_computation.5.clone.1 | loop fusion | flops 33030144 | bytes 6422784 | tf_op jit(solution)/shard_map/while/body/eval_jaxpr/tsnc,snc->tnc/dot_general | solution.py:59
  188.8 1.1 fusion.44
  192.1 1.7 fusion.19
  193.8 23.5 %all-gather.8.cloned.1.call-done = f32[128,2048]{1,0:T(8,128)} async-done(((f32[16,2048]{1,0:T(8,128)}), f32[128,2048]{1,0:T(8,128)}) %all-gather.8.cloned.1.call-update) | async-done | bytes 1048592 | tf_op jit(solution)/shard_map/all_gather | solution.py:17
  217.3 25.4 %all-gather.10.cloned.1.call-done = f32[128,2048]{1,0:T(8,128)} async-done(((f32[16,2048]{1,0:T(8,128)}), f32[128,2048]{1,0:T(8,128)}) %all-gather.10.cloned.1.call-update) | async-done | bytes 1048592 | tf_op jit(solution)/shard_map/all_gather | solution.py:17
  242.7 7.6 %while.30 = (s32[]{:T(128)}, f32[16,2048]{1,0:T(8,128)S(1)}, s32[]{:T(128)}, f32[8,16,2048]{2,1,0:T(8,128)}, f32[8,16,2048]{2,1,0:T(8,128)}, /*index=5*/s32[]{:T(128)}, s32[]{:T(128)}) while((s32[]{:T(128)}, f32[16,2048]{1,0:T(8,128)S(1)}, s32[]{:T(128)}, f32[8,16,2048]{2,1,0:T(8,128)}, f32[8,16,2048]{2,1,0:T(8,128)}, ...), condition=%wide.region_4.5_spmd.clone, body=%wide.region_3.4_spmd.clone.sunk | while | flops 131076 | bytes 524389 | solution.py:26
  242.7 1.1 fusion.39
  243.8 1.1 fusion.39
  244.9 1.1 fusion.39
  246.0 1.1 fusion.39
  247.1 1.1 fusion.39
  248.2 1.1 fusion.39
  249.3 1.1 fusion.39
  250.4 12.4 %fusion.9 = f32[128,1,2048]{2,1,0:T(1,128)S(1)} fusion(f32[128,16,1]{1,2,0:T(1,128)S(1)} %copy.22, f32[16,2048]{1,0:T(8,128)S(1)} %get-tuple-element.164, f32[16,2048]{1,0:T(8,128)S(1)} %get-tuple-element.439, f32[128,2048]{1,0:T(8,128)} %fusion.19), kind=kOutput, calls=%fused_computation.21 | convolution fusion | flops 58720256 | bytes 2367488 | tf_op jit(solution)/shard_map/tn,tnc->tc/dot_general | solution.py:130
  262.8 1.4 multiply_convert_fusion
  (117 shorter events, 16.1 us)
Async XLA Ops:
  6.5 45.4 %copy-start = (bf16[2048,288]{0,1:T(8,128)(2,1)S(1)}, bf16[2048,288]{0,1:T(8,128)(2,1)}, u32[]{:S(2)}) copy-start(bf16[2048,288]{0,1:T(8,128)(2,1)} %param.18) | copy-start | bytes 3538948
  6.5 31.4 %all-gather.6.cloned.1.call-start = ((), (), s32[]{:S(2)}) async-start(), calls=%async_computation | async-start | bytes 1310720 | tf_op jit(solution)/shard_map/all_gather | solution.py:95
  7.3 43.1 %copy-start.5 = (f32[4,2048]{1,0:T(4,128)S(1)}, f32[4,2048]{1,0:T(4,128)}, u32[]{:S(2)}) copy-start(f32[4,2048]{1,0:T(4,128)} %param.16) | copy-start | bytes 98308
  7.3 44.0 %copy-start.6 = (f32[2048]{0:T(1024)S(1)}, f32[2048]{0:T(1024)}, u32[]{:S(2)}) copy-start(f32[2048]{0:T(1024)} %param.17) | copy-start | bytes 24580
  7.3 78.5 %all-reduce.2.cloned.1.call-start = ((), (), s32[]{:S(2)}) async-start(), calls=%async_computation.1 | async-start | bytes 294912 | tf_op jit(solution)/shard_map/psum | solution.py:106
  46.4 6.8 %copy-start.4 = (f32[16,2048]{1,0:T(8,128)S(1)}, f32[16,2048]{1,0:T(8,128)}, u32[]{:S(2)}) copy-start(f32[16,2048]{1,0:T(8,128)} %param.21) | copy-start | bytes 393220
  46.4 40.3 %copy-start.7 = (f32[2048]{0:T(1024)S(1)}, f32[2048]{0:T(1024)}, u32[]{:S(2)}) copy-start(f32[2048]{0:T(1024)} %param.20) | copy-start | bytes 24580
  46.5 4.8 %collective-permute-start = (bf16[3,2048]{1,0:T(4,128)(2,1)S(1)}, bf16[3,2048]{1,0:T(4,128)(2,1)S(1)}, u32[]{:S(2)}, u32[]{:S(2)}) collective-permute-start(bf16[3,2048]{1,0:T(4,128)(2,1)S(1)} %slice.57), channel_id=1, source_target_pairs={{0,4},{4,8},{8,12},{12,16},{16,20},{20,24},{24,28},{1,5},{5,9},{9,... | collective-permute-start | bytes 36872 | tf_op jit(solution)/shard_map/ppermute | solution.py:12
  53.1 164.1 %all-gather.8.cloned.1.call-start = ((), (), s32[]{:S(2)}) async-start(), calls=%async_computation.2 | async-start | bytes 1179648 | tf_op jit(solution)/shard_map/all_gather | solution.py:17
  190.7 0.7 copy-start.2
  190.7 0.9 copy-start.1
  191.4 51.3 %all-gather.10.cloned.1.call-start = ((), (), s32[]{:S(2)}) async-start(), calls=%async_computation.3 | async-start | bytes 1179648 | tf_op jit(solution)/shard_map/all_gather | solution.py:17
  250.3 12.5 %copy-start.3 = (f32[8,16,2048]{2,1,0:T(8,128)S(1)}, f32[8,16,2048]{2,1,0:T(8,128)}, u32[]{:S(2)}) copy-start(f32[8,16,2048]{2,1,0:T(8,128)} %get-tuple-element.161) | copy-start | bytes 3145732
  250.3 12.5 %copy-start.8 = (f32[2048]{0:T(1024)S(1)}, f32[2048]{0:T(1024)}, u32[]{:S(2)}) copy-start(f32[2048]{0:T(1024)} %param.23) | copy-start | bytes 24580
  250.4 12.5 %copy-start.9 = (f32[2048]{0:T(1024)S(1)}, f32[2048]{0:T(1024)}, u32[]{:S(2)}) copy-start(f32[2048]{0:T(1024)} %param.22) | copy-start | bytes 24580
Sparse Core Ops, SparseCore 0:
  8.9 28.9 all-gather.5
  53.3 32.4 all-reduce.1
  191.5 25.7 all-gather.7
  219.2 23.4 all-gather.9
where the time goes:
time: 272 us; the launch traced here: 271 us
  waiting for transfers between devices  114 us (42%)
  other arithmetic  85.6 us (31%)
  matrix products  37.7 us (14%)
  local copies, waits for them, and re-layouts  15 us (6%)
  between operations  13.4 us (5%)
  starting transfers between devices  4.23 us (2%)
    dot_general x8, other arithmetic, run(): jnp.einsum('tsnc,snc->tnc', weights, inflow, precision=lax.Precision.HIGH...  69.4 us
    all_gather x2, waiting for transfers between devices, carried_in(): pieces = jax.tree.map(lambda part: lax.all_gather(part, axis), value)  48.9 us
    psum x1, waiting for transfers between devices, per_device(): total = lax.psum(partial_sums, 'tp')  32.5 us
    all_gather x1, waiting for transfers between devices, per_device(): lax.all_gather(tokens, 'tp', axis=1, tiled=True)  30.6 us
    dot_general x1, matrix products, per_device(): jnp.einsum('tn,tnc->tc', c_coef, growth * entry_state[None], precision=la...  12.4 us
    dot_general x8, matrix products, run(): jnp.einsum('tn,tnc->tc', c_block, states, precision=lax.Precision.HIGHEST)  8.93 us
    dot_general x1, matrix products, per_device(): jnp.dot(lax.all_gather(tokens, 'tp', axis=1, tiled=True), in_weight, pref...  8.44 us
    select_n x7, other arithmetic, turn(): jnp.where(position < mine, new, old)  7.49 us
  transfers between devices with their start and end apart: 5, of which 5 were waited for; matrix products, arithmetic and copies ran while one was open for 1% of the time, Pallas kernels for 0%

commit v1 on v0

v1 whole, which is shorter than its diff:
```python
import functools

import jax
import jax.numpy as jnp
from jax import lax
from jax.experimental import pallas as pl
from jax.experimental.pallas import tpu as pltpu
from jax.sharding import PartitionSpec as P

MESH = pl.DeviceIdType.MESH
LOG2E = 1.4426950408889634
LANES = 128
HALVES = 2


def kernel(
    ns,
    ntp,
    tok_ref,
    w_hbm,
    cw_ref,
    cb_ref,
    proj_ref,
    dtw_ref,
    dtb_ref,
    alog_ref,
    skip_ref,
    thr_ref,
    out_ref,
    w_ref,
    tok_all,
    acc,
    pad,
    halo_out,
    halo_in,
    u_ref,
    part,
    ps,
    rs,
    ag,
    tot,
    bs,
    dt3,
    du3,
    y3,
    r3,
    sx,
    sr,
    entry,
    w_sem,
    tok_recv,
    tok_right,
    tok_left,
    halo_sem,
    rs_send,
    rs_recv,
    ag_send,
    ag_recv,
    st_send,
    st_recv,
):
    q = lax.axis_index("seq")
    z = lax.axis_index("tp")
    rows, depth = tok_ref.shape
    width = w_ref.shape[1]
    taps = cw_ref.shape[0]
    rank = dtw_ref.shape[0]
    n_state = alog_ref.shape[0]
    cols = proj_ref.shape[1]
    tiles = width // LANES
    stride = r3.shape[0] // n_state
    groups = stride // 8
    piece = rows // HALVES
    per = rows // ntp
    f32, bf16 = jnp.float32, jnp.bfloat16

    def w_copy(k):
        part_k = pl.ds(pl.multiple_of(k * depth, depth), depth)
        return pltpu.make_async_copy(w_hbm.at[part_k], w_ref.at[part_k], w_sem.at[k])

    for i in range(ntp):
        w_copy(lax.rem(z + i, ntp)).start()

    barrier = pltpu.get_barrier_semaphore()
    for d in range(1, ntp):
        pl.semaphore_signal(
            barrier, inc=1, device_id={"tp": lax.rem(z + d, ntp)}, device_id_type=MESH
        )
    for d in range(1, ns):
        pl.semaphore_signal(
            barrier, inc=1, device_id={"seq": lax.rem(q + d, ns)}, device_id_type=MESH
        )
    pl.semaphore_wait(barrier, ns + ntp - 2)

    def tok_copy(k, h, by, sems, own):
        at = pl.ds(h * piece, piece)
        return pltpu.make_async_remote_copy(
            src_ref=tok_ref.at[at] if own else tok_all.at[k, at],
            dst_ref=tok_all.at[k, at],
            send_sem=sems.at[k, h],
            recv_sem=tok_recv.at[k, h],
            device_id={"tp": z + by},
            device_id_type=MESH,
        )

    for h in range(HALVES):

        @pl.when(z + 1 < ntp)
        def _():
            tok_copy(z, h, 1, tok_right, True).start()

        @pl.when(z > 0)
        def _():
            tok_copy(z, h, -1, tok_left, True).start()

    tn = min(512, width)

    def multiply(block, k, first):
        w_copy(k).wait()
        part_k = pl.ds(pl.multiple_of(k * depth, depth), depth)

        @pl.loop(0, width // tn)
        def _(i):
            at = pl.ds(pl.multiple_of(i * tn, tn), tn)
            got = jnp.dot(block[...], w_ref[part_k, at], preferred_element_type=f32)
            acc[:, at] = got if first else acc[:, at] + got

    for j in range(tiles):
        at = slice(j * LANES, (j + 1) * LANES)
        r3[pl.ds(j, n_state, stride=stride), :] = -LOG2E * jnp.exp(alog_ref[:, at])
    multiply(tok_ref, z, True)

    for d in range(1, ntp):
        for h in range(HALVES):

            @pl.when(z - d >= 0)
            def _():
                tok_copy(z - d, h, 1, tok_right, False).wait_recv()

                @pl.when(z + 1 < ntp)
                def _():
                    tok_copy(z - d, h, 1, tok_right, False).start()

            @pl.when(z + d < ntp)
            def _():
                tok_copy(z + d, h, -1, tok_left, False).wait_recv()

                @pl.when(z > 0)
                def _():
                    tok_copy(z + d, h, -1, tok_left, False).start()

        @pl.when(z - d >= 0)
        def _():
            multiply(tok_all.at[z - d], z - d, False)

        @pl.when(z + d < ntp)
        def _():
            multiply(tok_all.at[z + d], z + d, False)

    halo_out[...] = acc[rows - 16 :, :].astype(bf16)
    halo = pltpu.make_async_remote_copy(
        src_ref=halo_out,
        dst_ref=halo_in,
        send_sem=halo_sem.at[0],
        recv_sem=halo_sem.at[1],
        device_id={"seq": q + 1},
        device_id_type=MESH,
    )

    @pl.when(q + 1 < ns)
    def _():
        halo.start()

    pad[pl.ds(8, rows), :] = acc[...].astype(bf16).astype(f32)

    @pl.when(q > 0)
    def _():
        halo.wait_recv()
        pad[pl.ds(0, 8), :] = halo_in[...].astype(f32)[8:]

    @pl.when(q == 0)
    def _():
        pad[pl.ds(0, 8), :] = jnp.zeros((8, width), f32)

    for j in range(tiles):
        at = slice(j * LANES, (j + 1) * LANES)
        pre = cb_ref[:, at] + cw_ref[0:1, at] * pad[pl.ds(9 - taps, rows), at]
        for k in range(1, taps):
            pre = pre + cw_ref[k : k + 1, at] * pad[pl.ds(9 - taps + k, rows), at]
        u_ref[:, at] = (pre / (1.0 + jnp.exp(-pre))).astype(bf16)

    part[:, :cols] = jnp.dot(u_ref[...], proj_ref[...], preferred_element_type=f32)
    part[:, cols:] = jnp.zeros((rows, part.shape[1] - cols), f32)
    for k in range(ntp):
        ps[k] = part[k * per : (k + 1) * per, :].astype(bf16)

    def rs_copy(d):
        to = lax.rem(z + d, ntp)
        return pltpu.make_async_remote_copy(
            src_ref=ps.at[to],
            dst_ref=rs.at[d - 1],
            send_sem=rs_send.at[d - 1],
            recv_sem=rs_recv.at[d - 1],
            device_id={"tp": to},
            device_id_type=MESH,
        )

    def ag_copy(d):
        to = lax.rem(z + d, ntp)
        return pltpu.make_async_remote_copy(
            src_ref=ag.at[z],
            dst_ref=ag.at[z],
            send_sem=ag_send.at[d - 1],
            recv_sem=ag_recv.at[d - 1],
            device_id={"tp": to},
            device_id_type=MESH,
        )

    for d in range(1, ntp):
        rs_copy(d).start()
    red = part[pl.ds(pl.multiple_of(z * per, per), per), :]
    for d in range(1, ntp):
        rs_copy(d).wait_recv()
        red = red + rs[d - 1].astype(f32)
    ag[z] = red.astype(bf16)
    for d in range(1, ntp):
        ag_copy(d).start()
    for d in range(1, ntp):
        ag_copy(d).wait_recv()
    for k in range(ntp):
        tot[pl.ds(k * per, per), :] = ag[k].astype(f32)

    dt_low = tot[:, :rank].astype(bf16)
    for j0 in range(0, width, tn):
        at = slice(j0, j0 + tn)
        v = jnp.dot(dt_low, dtw_ref[:, at], preferred_element_type=f32) + dtb_ref[:, at]
        v = jnp.maximum(v, 0.0) + jnp.log1p(jnp.exp(-jnp.abs(v)))
        flow = v * u_ref[:, at].astype(f32)
        for i in range(tn // LANES):
            cut = slice(i * LANES, (i + 1) * LANES)
            to = pl.ds(j0 // LANES + i, rows, stride=stride)
            dt3[to, :] = v[:, cut]
            du3[to, :] = flow[:, cut]
    two = 2 * n_state
    for n in range(two):
        bs[pl.ds(n, rows, stride=two), :] = jnp.broadcast_to(
            tot[:, rank + n : rank + n + 1], (rows, LANES)
        )

    def rates(g):
        return [r3[pl.ds(n * stride + g * 8, 8), :] for n in range(n_state)]

    def splat(t, n):
        return jnp.broadcast_to(bs[pl.ds(t * two + n, 1), :], (8, LANES))

    def st_copy(g, d):
        return pltpu.make_async_remote_copy(
            src_ref=sx.at[g],
            dst_ref=sr.at[g, d - 1],
            send_sem=st_send.at[g, d - 1],
            recv_sem=st_recv.at[g, d - 1],
            device_id={"seq": q + d},
            device_id_type=MESH,
        )

    def first_pass(g):
        rate = rates(g)

        def step(t, carry):
            states, total = carry
            at = pl.ds(pl.multiple_of(t * stride + g * 8, 8), 8)
            dt, du = dt3[at, :], du3[at, :]
            states = [
                jnp.exp2(dt * rate[n]) * states[n] + du * splat(t, n) for n in range(n_state)
            ]
            return states, total + dt

        zero = jnp.zeros((8, LANES), f32)
        states, total = lax.fori_loop(0, rows, step, ([zero] * n_state, zero), unroll=4)
        high = total.astype(bf16).astype(f32)
        items = states + [high, total - high]
        for n in range(0, len(items), 2):
            sx[g, pl.ds(n * 8, 16), :] = jnp.concatenate(items[n : n + 2], axis=0).astype(bf16)
        for d in range(1, ns):

            @pl.when(q + d < ns)
            def _():
                st_copy(g, d).start()

    def second_pass(g):
        rate = rates(g)
        zero = jnp.zeros((8, LANES), f32)
        for n in range(n_state):
            entry[pl.ds(n * 8, 8), :] = zero
        for d in range(ns - 1, 0, -1):

            @pl.when(q - d >= 0)
            def _():
                st_copy(g, d).wait_recv()
                sums = sr[g, d - 1, pl.ds(n_state * 8, 16), :].astype(f32)
                sums = sums[:8] + sums[8:]
                for n in range(0, n_state, 2):
                    ends = sr[g, d - 1, pl.ds(n * 8, 16), :].astype(f32)
                    for i in range(2):
                        at = pl.ds((n + i) * 8, 8)
                        entry[at, :] = (
                            jnp.exp2(sums * rate[n + i]) * entry[at, :] + ends[i * 8 : i * 8 + 8]
                        )

        def step(t, states):
            at = pl.ds(pl.multiple_of(t * stride + g * 8, 8), 8)
            dt, du = dt3[at, :], du3[at, :]
            states = [
                jnp.exp2(dt * rate[n]) * states[n] + du * splat(t, n) for n in range(n_state)
            ]
            terms = [splat(t, n_state + n) * states[n] for n in range(n_state)]
            while len(terms) > 1:
                terms = [a + b for a, b in zip(terms[::2], terms[1::2])]
            y3[at, :] = terms[0]
            return states

        lax.fori_loop(0, rows, step, [entry[pl.ds(n * 8, 8), :] for n in range(n_state)], unroll=4)

    for g in range(groups):
        first_pass(g)
    for g in range(groups):
        second_pass(g)
        for j in range(g * 8, min(g * 8 + 8, tiles)):
            at = slice(j * LANES, (j + 1) * LANES)
            y = y3[pl.ds(j, rows, stride=stride), :] + skip_ref[:, at] * u_ref[:, at].astype(f32)
            out_ref[:, at] = (y / (1.0 + jnp.exp(-4.0 * (y - thr_ref[:, at])))).astype(bf16)

    for k in range(ntp):
        for h in range(HALVES):

            @pl.when((z + 1 < ntp) & (k <= z))
            def _():
                tok_copy(k, h, 1, tok_right, False).wait_send()

            @pl.when((z > 0) & (k >= z))
            def _():
                tok_copy(k, h, -1, tok_left, False).wait_send()

    @pl.when(q + 1 < ns)
    def _():
        halo.wait_send()

    for d in range(1, ntp):
        rs_copy(d).wait_send()
        ag_copy(d).wait_send()
    for g in range(groups):
        for d in range(1, ns):

            @pl.when(q + d < ns)
            def _():
                st_copy(g, d).wait_send()


def per_device(
    ns,
    ntp,
    tokens,
    in_weight,
    conv_weight,
    conv_bias,
    proj_weight,
    dt_weight,
    dt_bias,
    a_log,
    skip_gain,
    threshold,
):
    rows, depth = tokens.shape
    width = in_weight.shape[1]
    n_state = a_log.shape[0]
    stride = -(-width // (8 * LANES)) * 8
    groups = stride // 8
    padded = -(-proj_weight.shape[1] // LANES) * LANES
    per = rows // ntp
    f32, bf16 = jnp.float32, jnp.bfloat16
    dma = pltpu.SemaphoreType.DMA
    vmem = pl.BlockSpec(memory_space=pltpu.VMEM)
    return pl.pallas_call(
        functools.partial(kernel, ns, ntp),
        out_shape=jax.ShapeDtypeStruct((rows, width), bf16),
        in_specs=[vmem, pl.BlockSpec(memory_space=pl.ANY)] + [vmem] * 8,
        out_specs=vmem,
        scratch_shapes=[
            pltpu.VMEM(in_weight.shape, bf16),
            pltpu.VMEM((ntp, rows, depth), bf16),
            pltpu.VMEM((rows, width), f32),
            pltpu.VMEM((rows + 8, width), f32),
            pltpu.VMEM((16, width), bf16),
            pltpu.VMEM((16, width), bf16),
            pltpu.VMEM((rows, width), bf16),
            pltpu.VMEM((rows, padded), f32),
            pltpu.VMEM((ntp, per, padded), bf16),
            pltpu.VMEM((ntp - 1, per, padded), bf16),
            pltpu.VMEM((ntp, per, padded), bf16),
            pltpu.VMEM((rows, padded), f32),
            pltpu.VMEM((rows * 2 * n_state, LANES), f32),
            pltpu.VMEM((rows * stride, LANES), f32),
            pltpu.VMEM((rows * stride, LANES), f32),
            pltpu.VMEM((rows * stride, LANES), f32),
            pltpu.VMEM((n_state * stride, LANES), f32),
            pltpu.VMEM((groups, n_state * 8 + 16, LANES), bf16),
            pltpu.VMEM((groups, ns - 1, n_state * 8 + 16, LANES), bf16),
            pltpu.VMEM((n_state * 8, LANES), f32),
            dma((ntp,)),
            dma((ntp, HALVES)),
            dma((ntp, HALVES)),
            dma((ntp, HALVES)),
            dma((2,)),
            dma((ntp - 1,)),
            dma((ntp - 1,)),
            dma((ntp - 1,)),
            dma((ntp - 1,)),
            dma((groups, ns - 1)),
            dma((groups, ns - 1)),
        ],
        compiler_params=pltpu.CompilerParams(
            collective_id=0, has_side_effects=True, vmem_limit_bytes=48 * 1024 * 1024
        ),
    )(
        tokens,
        in_weight,
        conv_weight,
        conv_bias.reshape(1, -1),
        proj_weight,
        dt_weight,
        dt_bias.reshape(1, -1),
        a_log,
        skip_gain.reshape(1, -1),
        threshold.reshape(1, -1),
    )


def solution(mesh):
    return jax.shard_map(
        functools.partial(per_device, mesh.shape["seq"], mesh.shape["tp"]),
        mesh=mesh,
        in_specs=(
            P("seq", "tp"),
            P(None, "tp"),
            P(None, "tp"),
            P("tp"),
            P("tp", None),
            P(None, "tp"),
            P("tp"),
            P(None, "tp"),
            P("tp"),
            P("tp"),
        ),
        out_specs=P("seq", "tp"),
        check_vma=False,
    )
```

time: 272 us -> 53.4 us (0.20)
  waiting for transfers between devices: 114 us -> 0 us
  other arithmetic: 85.6 us -> 0 us
  Pallas kernels: 0 us -> 50.4 us
  matrix products: 37.7 us -> 0 us
  between operations: 13.4 us -> 0.12 us
  local copies, waits for them, and re-layouts: 15 us -> 2.75 us
  starting transfers between devices: 4.23 us -> 0 us
    all_gather x3 -> x0, waiting for transfers between devices: 79.6 us -> none  [the longest x2 48.9 us: carried_in(): pieces = jax.tree.map(lambda part: lax.all_gather(part, axis), value)]
    dot_general x8 -> x0, other arithmetic: 69.4 us -> none  [run(): jnp.einsum('tsnc,snc->tnc', weights, inflow, precision=lax.Precision.HIGH...]
    pallas_call x0 -> x1, Pallas kernels: none -> 50.4 us  [per_device(): pl.pallas_call(functools.partial(kernel, ns, ntp), out_shape=jax.ShapeDty...]
    dot_general x21 -> x0, matrix products: 37.7 us -> none  [the longest x1 12.4 us: per_device(): jnp.einsum('tn,tnc->tc', c_coef, growth * entry_state[None], precision=la...]
    psum x1 -> x0, waiting for transfers between devices: 32.5 us -> none  [per_device(): total = lax.psum(partial_sums, 'tp')]
    select_n x15 -> x0, other arithmetic: 10.7 us -> none  [the longest x7 7.49 us: turn(): jnp.where(position < mine, new, old)]
    mul x16 -> x0, local copies, waits for them, and re-layouts: 7.44 us -> none  [run(): inflow = flow_block[:, None, :] * b_block[:, :, None]]
    dynamic_update_slice x8 -> x0, local copies, waits for them, and re-layouts: 5.53 us -> none  [local_pass(): lax.scan(run, (start_state, jnp.ones_like(start_state)), items)]
  transfers between devices with their start and end apart: 5 -> 0, of which waited for: 5 -> 0; matrix products, arithmetic and copies ran while one was open for 1% -> 0% of each run, Pallas kernels for 0% -> 0%
where the time goes in v1:
time: 53.4 us; the launch traced here: 53.3 us
  Pallas kernels  50.4 us (94%)
  local copies, waits for them, and re-layouts  2.75 us (5%)
    pallas_call x1, Pallas kernels, per_device(): pl.pallas_call(functools.partial(kernel, ns, ntp), out_shape=jax.ShapeDty...  50.4 us
    unnamed x18, local copies, waits for them, and re-layouts  2.75 us

profile of v1, /device:TPU:5, one launch (start us, length us, event | category | flops | bytes accessed | tf_op | source)
XLA Modules:
  0.0 53.3 jit_solution(14819054279818929232)
XLA Ops:
  0.0 0.0 copy-start.7
  0.0 0.0 copy-start.6
  0.0 0.0 copy-start.2
  0.0 0.0 copy-start.5
  0.0 0.0 copy-start
  0.0 0.0 copy-start.4
  0.0 0.0 copy-start.3
  0.0 0.0 copy-start.1
  0.1 1.9 %copy.11.proj_ref = bf16[2048,288]{1,0:T(8,128)(2,1)S(1)} copy(bf16[2048,288]{0,1:T(8,128)(2,1)} %param.14) | data formatting | bytes 2359296 | tf_op args[4]
  2.0 0.0 copy-done.7
  2.0 0.0 copy-done.6
  2.0 0.0 copy-done.2
  2.0 0.0 copy-done.5
  2.0 0.0 copy-done
  2.0 0.0 copy-done.4
  2.0 0.0 copy-done.3
  2.1 0.0 copy-done.1
  2.1 50.4 %shard_map.100 = bf16[128,2048]{1,0:T(8,128)(2,1)S(1)} custom-call(bf16[128,1024]{1,0:T(8,128)(2,1)S(1)} %copy-done.1, bf16[4096,2048]{1,0:T(8,128)(2,1)} %w_hbm.1, f32[4,2048]{1,0:T(4,128)S(1)} %copy-done.3, f32[1,2048]{1,0:T(1,128)S(1)} %bitcast.4, bf16[2048,288]{1,0:T(8,128)(2,1)S(1)} %copy.11.proj_ref, bf16[256,2048]{1,0:T(8,128)(2,1)S(1)} %copy-done, ...), custom_call_target="tpu_custom_call" | custom-call | tf_op jit(solution)/shard_map/pallas_call | solution.py:383
  52.5 0.8 %copy.13 = bf16[128,2048]{1,0:T(8,128)(2,1)} copy(bf16[128,2048]{1,0:T(8,128)(2,1)S(1)} %shard_map.100) | data formatting | bytes 1048576
Async XLA Ops:
  0.0 2.0 %copy-start.7 = (f32[2048]{0:T(1024)S(1)}, f32[2048]{0:T(1024)}, u32[]{:S(2)}) copy-start(f32[2048]{0:T(1024)} %param.19) | copy-start | bytes 24580
  0.0 2.0 %copy-start.6 = (f32[2048]{0:T(1024)S(1)}, f32[2048]{0:T(1024)}, u32[]{:S(2)}) copy-start(f32[2048]{0:T(1024)} %param.18) | copy-start | bytes 24580
  0.0 2.0 %copy-start.2 = (f32[16,2048]{1,0:T(8,128)S(1)}, f32[16,2048]{1,0:T(8,128)}, u32[]{:S(2)}) copy-start(f32[16,2048]{1,0:T(8,128)} %alog_ref.1) | copy-start | bytes 393220
  0.0 2.0 %copy-start.5 = (f32[2048]{0:T(1024)S(1)}, f32[2048]{0:T(1024)}, u32[]{:S(2)}) copy-start(f32[2048]{0:T(1024)} %param.16) | copy-start | bytes 24580
  0.0 2.0 %copy-start = (bf16[256,2048]{1,0:T(8,128)(2,1)S(1)}, bf16[256,2048]{1,0:T(8,128)(2,1)}, u32[]{:S(2)}) copy-start(bf16[256,2048]{1,0:T(8,128)(2,1)} %dtw_ref.1) | copy-start | bytes 3145732
  0.0 2.0 %copy-start.4 = (f32[2048]{0:T(1024)S(1)}, f32[2048]{0:T(1024)}, u32[]{:S(2)}) copy-start(f32[2048]{0:T(1024)} %param.13) | copy-start | bytes 24580
  0.0 2.0 %copy-start.3 = (f32[4,2048]{1,0:T(4,128)S(1)}, f32[4,2048]{1,0:T(4,128)}, u32[]{:S(2)}) copy-start(f32[4,2048]{1,0:T(4,128)} %cw_ref.1) | copy-start | bytes 98308
  0.0 2.0 %copy-start.1 = (bf16[128,1024]{1,0:T(8,128)(2,1)S(1)}, bf16[128,1024]{1,0:T(8,128)(2,1)}, u32[]{:S(2)}) copy-start(bf16[128,1024]{1,0:T(8,128)(2,1)} %tok_ref.1) | copy-start | bytes 786436

commit v2 on v1

v2 whole, which is shorter than its diff:
```python
import functools

import jax
import jax.numpy as jnp
from jax import lax
from jax.experimental import pallas as pl
from jax.experimental.pallas import tpu as pltpu
from jax.sharding import PartitionSpec as P

MESH = pl.DeviceIdType.MESH
LOG2E = 1.4426950408889634
LANES = 128


def kernel(
    ns,
    ntp,
    tok_hbm,
    w_hbm,
    cw_hbm,
    cb_hbm,
    proj_hbm,
    dtw_hbm,
    dtb_hbm,
    alog_hbm,
    skip_hbm,
    thr_hbm,
    out_ref,
    w_ref,
    cw_ref,
    cb_ref,
    proj_ref,
    dtw_ref,
    dtb_ref,
    alog_ref,
    skip_ref,
    thr_ref,
    tok_all,
    acc,
    pad,
    halo_out,
    halo_in,
    u_ref,
    part,
    ps,
    rs,
    ag,
    tot,
    bs,
    dt3,
    du3,
    y3,
    r3,
    later,
    sx,
    sr,
    entry,
    w_sem,
    in_sem,
    tok_recv,
    tok_right,
    tok_left,
    halo_sem,
    rs_send,
    rs_recv,
    ag_send,
    ag_recv,
    st_send,
    st_recv,
):
    q = lax.axis_index("seq")
    z = lax.axis_index("tp")
    rows, depth = tok_hbm.shape
    width = w_ref.shape[1]
    taps = cw_ref.shape[0]
    rank = dtw_ref.shape[0]
    n_state = alog_ref.shape[0]
    cols = proj_ref.shape[0]
    tiles = width // LANES
    stride = r3.shape[0] // n_state
    groups = stride // 8
    per = ag.shape[2]
    f32, bf16 = jnp.float32, jnp.bfloat16
    half = rows // 2
    split = half - 16
    token_rows = ((split, rows - split), (0, split))
    phase_rows = (half, 0)

    small = [
        (cw_hbm, cw_ref),
        (cb_hbm, cb_ref),
        (proj_hbm, proj_ref),
        (dtw_hbm, dtw_ref),
        (dtb_hbm, dtb_ref),
        (alog_hbm, alog_ref),
        (skip_hbm, skip_ref),
        (thr_hbm, thr_ref),
        (tok_hbm, tok_all.at[z]),
    ]

    def in_copy(i):
        return pltpu.make_async_copy(small[i][0], small[i][1], in_sem.at[i])

    def w_copy(k):
        part_k = pl.ds(pl.multiple_of(k * depth, depth), depth)
        return pltpu.make_async_copy(w_hbm.at[part_k], w_ref.at[part_k], w_sem.at[k])

    in_copy(8).start()
    w_copy(z).start()

    barrier = pltpu.get_barrier_semaphore()
    for d in range(1, ntp):
        pl.semaphore_signal(
            barrier, inc=1, device_id={"tp": lax.rem(z + d, ntp)}, device_id_type=MESH
        )
    for d in range(1, ns):
        pl.semaphore_signal(
            barrier, inc=1, device_id={"seq": lax.rem(q + d, ns)}, device_id_type=MESH
        )
    for i in (5, 0, 1, 2, 3, 4, 6, 7):
        in_copy(i).start()
    for i in range(1, ntp):
        w_copy(lax.rem(z + i, ntp)).start()
    pl.semaphore_wait(barrier, ns + ntp - 2)

    def tok_copy(k, h, by, sems, own):
        at = pl.ds(*token_rows[h])
        return pltpu.make_async_remote_copy(
            src_ref=tok_hbm.at[at] if own else tok_all.at[k, at],
            dst_ref=tok_all.at[k, at],
            send_sem=sems.at[k, h],
            recv_sem=tok_recv.at[k, h],
            device_id={"tp": z + by},
            device_id_type=MESH,
        )

    def send_own(h):
        @pl.when(z + 1 < ntp)
        def _():
            tok_copy(z, h, 1, tok_right, True).start()

        @pl.when(z > 0)
        def _():
            tok_copy(z, h, -1, tok_left, True).start()

    def take(d, h):
        @pl.when(z - d >= 0)
        def _():
            tok_copy(z - d, h, 1, tok_right, False).wait_recv()

            @pl.when(z + 1 < ntp)
            def _():
                tok_copy(z - d, h, 1, tok_right, False).start()

        @pl.when(z + d < ntp)
        def _():
            tok_copy(z + d, h, -1, tok_left, False).wait_recv()

            @pl.when(z > 0)
            def _():
                tok_copy(z + d, h, -1, tok_left, False).start()

    tn = min(512, width)

    def multiply(k, h, first):
        if h == 0:
            w_copy(k).wait()
        part_k = pl.ds(pl.multiple_of(k * depth, depth), depth)
        mine = pl.ds(*token_rows[h])

        @pl.loop(0, width // tn)
        def _(i):
            at = pl.ds(pl.multiple_of(i * tn, tn), tn)
            got = jnp.dot(tok_all[k, mine, :], w_ref[part_k, at], preferred_element_type=f32)
            acc[mine, at] = got if first else acc[mine, at] + got

    def multiply_pair(d, h):
        @pl.when(z - d >= 0)
        def _():
            multiply(z - d, h, False)

        @pl.when(z + d < ntp)
        def _():
            multiply(z + d, h, False)

    halo = pltpu.make_async_remote_copy(
        src_ref=halo_out,
        dst_ref=halo_in,
        send_sem=halo_sem.at[0],
        recv_sem=halo_sem.at[1],
        device_id={"seq": q + 1},
        device_id_type=MESH,
    )

    def rs_copy(p, d):
        to = lax.rem(z + d, ntp)
        return pltpu.make_async_remote_copy(
            src_ref=ps.at[p, to],
            dst_ref=rs.at[p, d - 1],
            send_sem=rs_send.at[p, d - 1],
            recv_sem=rs_recv.at[p, d - 1],
            device_id={"tp": to},
            device_id_type=MESH,
        )

    def ag_copy(p, d):
        to = lax.rem(z + d, ntp)
        return pltpu.make_async_remote_copy(
            src_ref=ag.at[p, z],
            dst_ref=ag.at[p, z],
            send_sem=ag_send.at[p, d - 1],
            recv_sem=ag_recv.at[p, d - 1],
            device_id={"tp": to},
            device_id_type=MESH,
        )

    def project(p):
        r0 = phase_rows[p]
        for j in range(tiles):
            at = slice(j * LANES, (j + 1) * LANES)
            pre = cb_ref[:, at] + cw_ref[0:1, at] * pad[pl.ds(r0 + 9 - taps, half), at]
            for k in range(1, taps):
                pre = pre + cw_ref[k : k + 1, at] * pad[pl.ds(r0 + 9 - taps + k, half), at]
            u_ref[pl.ds(r0, half), at] = (pre / (1.0 + jnp.exp(-pre))).astype(bf16)
        sums = lax.dot_general(
            u_ref[pl.ds(r0, half), :],
            proj_ref[...],
            (((1,), (1,)), ((), ())),
            preferred_element_type=f32,
        )
        for k in range(ntp):
            mine = sums[k * per : (k + 1) * per]
            part[p, k, :, :cols] = mine
            ps[p, k, :, :cols] = mine.astype(ps.dtype)
        for d in range(1, ntp):
            rs_copy(p, d).start()

    def reduce(p):
        red = part[p, z]
        for d in range(1, ntp):
            rs_copy(p, d).wait_recv()
            red = red + rs[p, d - 1].astype(f32)
        ag[p, z] = red.astype(ag.dtype)
        for d in range(1, ntp):
            ag_copy(p, d).start()

    two = 2 * n_state

    def prepare(p):
        r0 = phase_rows[p]
        mine = pl.ds(r0, half)
        for d in range(1, ntp):
            ag_copy(p, d).wait_recv()
        for k in range(ntp):
            tot[pl.ds(r0 + k * per, per), :] = ag[p, k].astype(f32)
        dt_low = tot[mine, :rank].astype(bf16)
        for j0 in range(0, width, tn):
            at = slice(j0, j0 + tn)
            v = jnp.dot(dt_low, dtw_ref[:, at], preferred_element_type=f32) + dtb_ref[:, at]
            v = jnp.maximum(v, 0.0) + jnp.log1p(jnp.exp(-jnp.abs(v)))
            flow = v * u_ref[mine, at].astype(f32)
            for i in range(tn // LANES):
                cut = slice(i * LANES, (i + 1) * LANES)
                to = pl.ds(r0 * stride + j0 // LANES + i, half, stride=stride)
                dt3[to, :] = v[:, cut]
                du3[to, :] = flow[:, cut]
        for n in range(two):
            bs[pl.ds(r0 * two + n, half, stride=two), :] = jnp.broadcast_to(
                tot[mine, rank + n : rank + n + 1], (half, LANES)
            )

    def rates(g):
        return [r3[pl.ds(n * stride + g * 8, 8), :] for n in range(n_state)]

    def splat(t, n):
        return jnp.broadcast_to(bs[pl.ds(t * two + n, 1), :], (8, LANES))

    def st_copy(g, d):
        return pltpu.make_async_remote_copy(
            src_ref=sx.at[g],
            dst_ref=sr.at[g, d - 1],
            send_sem=st_send.at[g, d - 1],
            recv_sem=st_recv.at[g, d - 1],
            device_id={"seq": q + d},
            device_id_type=MESH,
        )

    def first_pass(p, g):
        rate = rates(g)
        r0 = phase_rows[p]

        def step(t, carry):
            states, total = carry
            at = pl.ds(pl.multiple_of(t * stride + g * 8, 8), 8)
            dt, du = dt3[at, :], du3[at, :]
            states = [
                jnp.exp2(dt * rate[n]) * states[n] + du * splat(t, n) for n in range(n_state)
            ]
            return states, total + dt

        zero = jnp.zeros((8, LANES), f32)
        states, total = lax.fori_loop(
            r0, r0 + half, step, ([zero] * n_state, zero), unroll=4
        )
        if p == 0:
            for n in range(n_state):
                later[g, pl.ds(n * 8, 8), :] = states[n]
            later[g, pl.ds(n_state * 8, 8), :] = total
            return
        more = later[g, pl.ds(n_state * 8, 8), :]
        states = [
            jnp.exp2(more * rate[n]) * states[n] + later[g, pl.ds(n * 8, 8), :]
            for n in range(n_state)
        ]
        total = total + more
        high = total.astype(bf16).astype(f32)
        items = states + [high, total - high]
        for n in range(0, len(items), 2):
            sx[g, pl.ds(n * 8, 16), :] = jnp.concatenate(items[n : n + 2], axis=0).astype(bf16)
        for d in range(1, ns):

            @pl.when(q + d < ns)
            def _():
                st_copy(g, d).start()

    def second_pass(g):
        rate = rates(g)
        zero = jnp.zeros((8, LANES), f32)
        for n in range(n_state):
            entry[pl.ds(n * 8, 8), :] = zero
        for d in range(ns - 1, 0, -1):

            @pl.when(q - d >= 0)
            def _():
                st_copy(g, d).wait_recv()
                sums = sr[g, d - 1, pl.ds(n_state * 8, 16), :].astype(f32)
                sums = sums[:8] + sums[8:]
                for n in range(0, n_state, 2):
                    ends = sr[g, d - 1, pl.ds(n * 8, 16), :].astype(f32)
                    for i in range(2):
                        at = pl.ds((n + i) * 8, 8)
                        entry[at, :] = (
                            jnp.exp2(sums * rate[n + i]) * entry[at, :] + ends[i * 8 : i * 8 + 8]
                        )

        def step(t, states):
            at = pl.ds(pl.multiple_of(t * stride + g * 8, 8), 8)
            dt, du = dt3[at, :], du3[at, :]
            states = [
                jnp.exp2(dt * rate[n]) * states[n] + du * splat(t, n) for n in range(n_state)
            ]
            terms = [splat(t, n_state + n) * states[n] for n in range(n_state)]
            while len(terms) > 1:
                terms = [a + b for a, b in zip(terms[::2], terms[1::2])]
            y3[at, :] = terms[0]
            return states

        lax.fori_loop(0, rows, step, [entry[pl.ds(n * 8, 8), :] for n in range(n_state)], unroll=4)
        for j in range(g * 8, min(g * 8 + 8, tiles)):
            at = slice(j * LANES, (j + 1) * LANES)
            y = y3[pl.ds(j, rows, stride=stride), :] + skip_ref[:, at] * u_ref[:, at].astype(f32)
            out_ref[:, at] = (y / (1.0 + jnp.exp(-4.0 * (y - thr_ref[:, at])))).astype(bf16)

    send_own(0)
    in_copy(8).wait()
    in_copy(5).wait()
    for j in range(tiles):
        at = slice(j * LANES, (j + 1) * LANES)
        r3[pl.ds(j, n_state, stride=stride), :] = -LOG2E * jnp.exp(alog_ref[:, at])
    part[:, :, :, cols:] = jnp.zeros(part.shape[:3] + (part.shape[3] - cols,), f32)
    ps[:, :, :, cols:] = jnp.zeros(ps.shape[:3] + (ps.shape[3] - cols,), ps.dtype)
    send_own(1)
    multiply(z, 0, True)
    for d in range(1, ntp):
        take(d, 0)
        multiply_pair(d, 0)
        if d < ntp - 1:
            take(d, 1)
    halo_out[...] = acc[rows - 16 :, :].astype(bf16)

    @pl.when(q + 1 < ns)
    def _():
        halo.start()

    pad[pl.ds(8 + split, rows - split), :] = acc[split:, :].astype(bf16).astype(f32)
    for i in (0, 1, 2):
        in_copy(i).wait()
    project(0)

    multiply(z, 1, True)
    for d in range(1, ntp - 1):
        multiply_pair(d, 1)
    reduce(0)
    if ntp > 1:
        take(ntp - 1, 1)
        multiply_pair(ntp - 1, 1)
    pad[pl.ds(8, split), :] = acc[:split, :].astype(bf16).astype(f32)

    @pl.when(q > 0)
    def _():
        halo.wait_recv()
        pad[pl.ds(0, 8), :] = halo_in[...].astype(f32)[8:]

    @pl.when(q == 0)
    def _():
        pad[pl.ds(0, 8), :] = jnp.zeros((8, width), f32)

    project(1)

    in_copy(3).wait()
    in_copy(4).wait()
    prepare(0)
    reduce(1)
    for g in range(groups):
        first_pass(0, g)
    prepare(1)
    for g in range(groups):
        first_pass(1, g)
    in_copy(6).wait()
    in_copy(7).wait()
    for g in range(groups):
        second_pass(g)

    for k in range(ntp):
        for h in range(2):

            @pl.when((z + 1 < ntp) & (k <= z))
            def _():
                tok_copy(k, h, 1, tok_right, False).wait_send()

            @pl.when((z > 0) & (k >= z))
            def _():
                tok_copy(k, h, -1, tok_left, False).wait_send()

    @pl.when(q + 1 < ns)
    def _():
        halo.wait_send()

    for p in range(2):
        for d in range(1, ntp):
            rs_copy(p, d).wait_send()
            ag_copy(p, d).wait_send()
    for g in range(groups):
        for d in range(1, ns):

            @pl.when(q + d < ns)
            def _():
                st_copy(g, d).wait_send()


def per_device(
    ns,
    ntp,
    tokens,
    in_weight,
    conv_weight,
    conv_bias,
    proj_weight,
    dt_weight,
    dt_bias,
    a_log,
    skip_gain,
    threshold,
):
    rows, depth = tokens.shape
    width = in_weight.shape[1]
    n_state = a_log.shape[0]
    stride = -(-width // (8 * LANES)) * 8
    groups = stride // 8
    padded = -(-proj_weight.shape[1] // LANES) * LANES
    per = rows // 2 // ntp
    f32, bf16 = jnp.float32, jnp.bfloat16
    sent = bf16 if per % 16 == 0 else f32
    dma = pltpu.SemaphoreType.DMA
    vmem = pl.BlockSpec(memory_space=pltpu.VMEM)
    return pl.pallas_call(
        functools.partial(kernel, ns, ntp),
        out_shape=jax.ShapeDtypeStruct((rows, width), bf16),
        in_specs=[pl.BlockSpec(memory_space=pl.ANY)] * 10,
        out_specs=vmem,
        scratch_shapes=[
            pltpu.VMEM(in_weight.shape, bf16),
            pltpu.VMEM(conv_weight.shape, f32),
            pltpu.VMEM((1, width), f32),
            pltpu.VMEM(proj_weight.shape[::-1], bf16),
            pltpu.VMEM(dt_weight.shape, bf16),
            pltpu.VMEM((1, width), f32),
            pltpu.VMEM(a_log.shape, f32),
            pltpu.VMEM((1, width), f32),
            pltpu.VMEM((1, width), f32),
            pltpu.VMEM((ntp, rows, depth), bf16),
            pltpu.VMEM((rows, width), f32),
            pltpu.VMEM((rows + 8, width), f32),
            pltpu.VMEM((16, width), bf16),
            pltpu.VMEM((16, width), bf16),
            pltpu.VMEM((rows, width), bf16),
            pltpu.VMEM((2, ntp, per, padded), f32),
            pltpu.VMEM((2, ntp, per, padded), sent),
            pltpu.VMEM((2, ntp - 1, per, padded), sent),
            pltpu.VMEM((2, ntp, per, padded), sent),
            pltpu.VMEM((rows, padded), f32),
            pltpu.VMEM((rows * 2 * n_state, LANES), f32),
            pltpu.VMEM((rows * stride, LANES), f32),
            pltpu.VMEM((rows * stride, LANES), f32),
            pltpu.VMEM((rows * stride, LANES), f32),
            pltpu.VMEM((n_state * stride, LANES), f32),
            pltpu.VMEM((groups, n_state * 8 + 8, LANES), f32),
            pltpu.VMEM((groups, n_state * 8 + 16, LANES), bf16),
            pltpu.VMEM((groups, ns - 1, n_state * 8 + 16, LANES), bf16),
            pltpu.VMEM((n_state * 8, LANES), f32),
            dma((ntp,)),
            dma((9,)),
            dma((ntp, 2)),
            dma((ntp, 2)),
            dma((ntp, 2)),
            dma((2,)),
            dma((2, ntp - 1)),
            dma((2, ntp - 1)),
            dma((2, ntp - 1)),
            dma((2, ntp - 1)),
            dma((groups, ns - 1)),
            dma((groups, ns - 1)),
        ],
        compiler_params=pltpu.CompilerParams(
            collective_id=0, has_side_effects=True, vmem_limit_bytes=63 * 1024 * 1024
        ),
    )(
        tokens,
        in_weight,
        conv_weight,
        conv_bias.reshape(1, -1),
        proj_weight.T,
        dt_weight,
        dt_bias.reshape(1, -1),
        a_log,
        skip_gain.reshape(1, -1),
        threshold.reshape(1, -1),
    )


def solution(mesh):
    return jax.shard_map(
        functools.partial(per_device, mesh.shape["seq"], mesh.shape["tp"]),
        mesh=mesh,
        in_specs=(
            P("seq", "tp"),
            P(None, "tp"),
            P(None, "tp"),
            P("tp"),
            P("tp", None),
            P(None, "tp"),
            P("tp"),
            P(None, "tp"),
            P("tp"),
            P("tp"),
        ),
        out_specs=P("seq", "tp"),
        check_vma=False,
    )
```

time: 53.4 us -> 53.1 us (level)
  local copies, waits for them, and re-layouts: 2.75 us -> 1.88 us
  Pallas kernels: 50.4 us -> 51 us
    unnamed x18 -> x1, local copies, waits for them, and re-layouts: 2.75 us -> 1.88 us
    pallas_call x1, Pallas kernels: 50.4 us -> 51 us  [per_device(): pl.pallas_call(functools.partial(kernel, ns, ntp), out_shape=jax.ShapeDty...]
where the time goes in v2:
time: 53.1 us; the launch traced here: 52.9 us
  Pallas kernels  51 us (96%)
  local copies, waits for them, and re-layouts  1.88 us (4%)
    pallas_call x1, Pallas kernels, per_device(): pl.pallas_call(functools.partial(kernel, ns, ntp), out_shape=jax.ShapeDty...  51 us
    unnamed x1, local copies, waits for them, and re-layouts  1.88 us

profile of v2, /device:TPU:5, one launch (start us, length us, event | category | flops | bytes accessed | tf_op | source)
XLA Modules:
  0.0 52.9 jit_solution(5725006599934840765)
XLA Ops:
  0.0 51.0 %shard_map.100 = bf16[128,2048]{1,0:T(8,128)(2,1)} custom-call(bf16[128,1024]{1,0:T(8,128)(2,1)} %tok_hbm.1, bf16[4096,2048]{1,0:T(8,128)(2,1)} %w_hbm.1, f32[4,2048]{1,0:T(4,128)} %cw_hbm.1, f32[1,2048]{1,0:T(1,128)} %bitcast.6, bf16[288,2048]{1,0:T(8,128)(2,1)} %bitcast.5, bf16[256,2048]{1,0:T(8,128)(2,1)} %dtw_hbm.1, f32[1,2048]{1,0:T(1,128)} %bitcast.7, ...), custom_call_target="tpu_custom_call" | custom-call | tf_op jit(solution)/shard_map/pallas_call | solution.py:476
  51.0 1.9 %copy.12 = bf16[128,2048]{1,0:T(8,128)(2,1)} copy(bf16[128,2048]{1,0:T(8,128)(2,1)} %shard_map.100) | data formatting | bytes 1048576

commit v3 on v2

--- a/solution.py
+++ b/solution.py
@@ -273,7 +273,7 @@
         return [r3[pl.ds(n * stride + g * 8, 8), :] for n in range(n_state)]
 
     def splat(t, n):
-        return jnp.broadcast_to(bs[pl.ds(t * two + n, 1), :], (8, LANES))
+        return bs[pl.ds(t * two + n, 8, stride=0), :]
 
     def st_copy(g, d):
         return pltpu.make_async_remote_copy(
@@ -300,7 +300,7 @@
 
         zero = jnp.zeros((8, LANES), f32)
         states, total = lax.fori_loop(
-            r0, r0 + half, step, ([zero] * n_state, zero), unroll=4
+            r0, r0 + half, step, ([zero] * n_state, zero), unroll=16
         )
         if p == 0:
             for n in range(n_state):
@@ -355,7 +355,7 @@
             y3[at, :] = terms[0]
             return states
 
-        lax.fori_loop(0, rows, step, [entry[pl.ds(n * 8, 8), :] for n in range(n_state)], unroll=4)
+        lax.fori_loop(0, rows, step, [entry[pl.ds(n * 8, 8), :] for n in range(n_state)], unroll=16)
         for j in range(g * 8, min(g * 8 + 8, tiles)):
             at = slice(j * LANES, (j + 1) * LANES)
             y = y3[pl.ds(j, rows, stride=stride), :] + skip_ref[:, at] * u_ref[:, at].astype(f32)
@@ -499,7 +499,7 @@
             pltpu.VMEM((2, ntp - 1, per, padded), sent),
             pltpu.VMEM((2, ntp, per, padded), sent),
             pltpu.VMEM((rows, padded), f32),
-            pltpu.VMEM((rows * 2 * n_state, LANES), f32),
+            pltpu.VMEM((rows * 2 * n_state + 8, LANES), f32),
             pltpu.VMEM((rows * stride, LANES), f32),
             pltpu.VMEM((rows * stride, LANES), f32),
             pltpu.VMEM((rows * stride, LANES), f32),

time: 53.1 us -> 52.5 us (0.989)
  Pallas kernels: 51 us -> 50.4 us
    pallas_call x1, Pallas kernels: 51 us -> 50.4 us  [per_device(): pl.pallas_call(functools.partial(kernel, ns, ntp), out_shape=jax.ShapeDty...]
where the time goes in v3:
time: 52.5 us; the launch traced here: 52.3 us
  Pallas kernels  50.4 us (96%)
  local copies, waits for them, and re-layouts  1.88 us (4%)
    pallas_call x1, Pallas kernels, per_device(): pl.pallas_call(functools.partial(kernel, ns, ntp), out_shape=jax.ShapeDty...  50.4 us
    unnamed x1, local copies, waits for them, and re-layouts  1.88 us

profile of v3, /device:TPU:5, one launch (start us, length us, event | category | flops | bytes accessed | tf_op | source)
XLA Modules:
  0.0 52.3 jit_solution(13608305748016485280)
XLA Ops:
  0.0 50.4 %shard_map.100 = bf16[128,2048]{1,0:T(8,128)(2,1)} custom-call(bf16[128,1024]{1,0:T(8,128)(2,1)} %tok_hbm.1, bf16[4096,2048]{1,0:T(8,128)(2,1)} %w_hbm.1, f32[4,2048]{1,0:T(4,128)} %cw_hbm.1, f32[1,2048]{1,0:T(1,128)} %bitcast.6, bf16[288,2048]{1,0:T(8,128)(2,1)} %bitcast.5, bf16[256,2048]{1,0:T(8,128)(2,1)} %dtw_hbm.1, f32[1,2048]{1,0:T(1,128)} %bitcast.7, ...), custom_call_target="tpu_custom_call" | custom-call | tf_op jit(solution)/shard_map/pallas_call | solution.py:476
  50.4 1.9 %copy.12 = bf16[128,2048]{1,0:T(8,128)(2,1)} copy(bf16[128,2048]{1,0:T(8,128)(2,1)} %shard_map.100) | data formatting | bytes 1048576

commit v4 on v3

--- a/solution.py
+++ b/solution.py
@@ -98,6 +98,12 @@
         (tok_hbm, tok_all.at[z]),
     ]
 
+    def tile_at(j):
+        return pl.ds(pl.multiple_of(j * LANES, LANES), LANES)
+
+    def sigmoid(v):
+        return 0.5 + 0.5 * jnp.tanh(0.5 * v)
+
     def in_copy(i):
         return pltpu.make_async_copy(small[i][0], small[i][1], in_sem.at[i])
 
@@ -216,12 +222,15 @@
 
     def project(p):
         r0 = phase_rows[p]
-        for j in range(tiles):
-            at = slice(j * LANES, (j + 1) * LANES)
+
+        @pl.loop(0, tiles)
+        def _(j):
+            at = tile_at(j)
             pre = cb_ref[:, at] + cw_ref[0:1, at] * pad[pl.ds(r0 + 9 - taps, half), at]
             for k in range(1, taps):
                 pre = pre + cw_ref[k : k + 1, at] * pad[pl.ds(r0 + 9 - taps + k, half), at]
-            u_ref[pl.ds(r0, half), at] = (pre / (1.0 + jnp.exp(-pre))).astype(bf16)
+            u_ref[pl.ds(r0, half), at] = (pre * sigmoid(pre)).astype(bf16)
+
         sums = lax.dot_general(
             u_ref[pl.ds(r0, half), :],
             proj_ref[...],
@@ -254,26 +263,33 @@
         for k in range(ntp):
             tot[pl.ds(r0 + k * per, per), :] = ag[p, k].astype(f32)
         dt_low = tot[mine, :rank].astype(bf16)
-        for j0 in range(0, width, tn):
-            at = slice(j0, j0 + tn)
+
+        @pl.loop(0, width // tn)
+        def _(s):
+            at = pl.ds(pl.multiple_of(s * tn, tn), tn)
             v = jnp.dot(dt_low, dtw_ref[:, at], preferred_element_type=f32) + dtb_ref[:, at]
-            v = jnp.maximum(v, 0.0) + jnp.log1p(jnp.exp(-jnp.abs(v)))
+            e = jnp.exp(-jnp.abs(v))
+            e = jnp.where(e < 1e-3, e - (0.5 * e) * e, jnp.log(1.0 + e))
+            v = jnp.maximum(v, 0.0) + e
             flow = v * u_ref[mine, at].astype(f32)
             for i in range(tn // LANES):
                 cut = slice(i * LANES, (i + 1) * LANES)
-                to = pl.ds(r0 * stride + j0 // LANES + i, half, stride=stride)
+                to = pl.ds(r0 * stride + s * (tn // LANES) + i, half, stride=stride)
                 dt3[to, :] = v[:, cut]
                 du3[to, :] = flow[:, cut]
+
         for n in range(two):
-            bs[pl.ds(r0 * two + n, half, stride=two), :] = jnp.broadcast_to(
+            bs[pl.ds(n * rows + r0, half), :] = jnp.broadcast_to(
                 tot[mine, rank + n : rank + n + 1], (half, LANES)
             )
 
     def rates(g):
-        return [r3[pl.ds(n * stride + g * 8, 8), :] for n in range(n_state)]
+        return [
+            r3[pl.ds(pl.multiple_of(n * stride + g * 8, 8), 8), :] for n in range(n_state)
+        ]
 
     def splat(t, n):
-        return bs[pl.ds(t * two + n, 8, stride=0), :]
+        return bs[pl.ds(n * rows + t, 8, stride=0), :]
 
     def st_copy(g, d):
         return pltpu.make_async_remote_copy(
@@ -300,7 +316,7 @@
 
         zero = jnp.zeros((8, LANES), f32)
         states, total = lax.fori_loop(
-            r0, r0 + half, step, ([zero] * n_state, zero), unroll=16
+            r0, r0 + half, step, ([zero] * n_state, zero), unroll=8
         )
         if p == 0:
             for n in range(n_state):
@@ -355,11 +371,13 @@
             y3[at, :] = terms[0]
             return states
 
-        lax.fori_loop(0, rows, step, [entry[pl.ds(n * 8, 8), :] for n in range(n_state)], unroll=16)
-        for j in range(g * 8, min(g * 8 + 8, tiles)):
-            at = slice(j * LANES, (j + 1) * LANES)
+        lax.fori_loop(0, rows, step, [entry[pl.ds(n * 8, 8), :] for n in range(n_state)], unroll=8)
+
+        @pl.loop(g * 8, jnp.minimum(g * 8 + 8, tiles))
+        def _(j):
+            at = tile_at(j)
             y = y3[pl.ds(j, rows, stride=stride), :] + skip_ref[:, at] * u_ref[:, at].astype(f32)
-            out_ref[:, at] = (y / (1.0 + jnp.exp(-4.0 * (y - thr_ref[:, at])))).astype(bf16)
+            out_ref[:, at] = (y * sigmoid(4.0 * (y - thr_ref[:, at]))).astype(bf16)
 
     send_own(0)
     in_copy(8).wait()
@@ -371,11 +389,16 @@
     ps[:, :, :, cols:] = jnp.zeros(ps.shape[:3] + (ps.shape[3] - cols,), ps.dtype)
     send_own(1)
     multiply(z, 0, True)
-    for d in range(1, ntp):
+
+    @pl.loop(1, ntp)
+    def _(d):
         take(d, 0)
         multiply_pair(d, 0)
-        if d < ntp - 1:
+
+        @pl.when(d < ntp - 1)
+        def _():
             take(d, 1)
+
     halo_out[...] = acc[rows - 16 :, :].astype(bf16)
 
     @pl.when(q + 1 < ns)
@@ -388,8 +411,11 @@
     project(0)
 
     multiply(z, 1, True)
-    for d in range(1, ntp - 1):
+
+    @pl.loop(1, ntp - 1)
+    def _(d):
         multiply_pair(d, 1)
+
     reduce(0)
     if ntp > 1:
         take(ntp - 1, 1)
@@ -411,15 +437,24 @@
     in_copy(4).wait()
     prepare(0)
     reduce(1)
-    for g in range(groups):
+
+    @pl.loop(0, groups)
+    def _(g):
         first_pass(0, g)
+
     prepare(1)
-    for g in range(groups):
+
+    @pl.loop(0, groups)
+    def _(g):
         first_pass(1, g)
+
     in_copy(6).wait()
     in_copy(7).wait()
-    for g in range(groups):
+
+    @pl.loop(0, groups)
+    def _(g):
         second_pass(g)
+
 
     for k in range(ntp):
         for h in range(2):

time: 52.5 us -> 53.9 us (1.027)
  Pallas kernels: 50.4 us -> 51.8 us
    pallas_call x1, Pallas kernels: 50.4 us -> 51.8 us  [per_device(): pl.pallas_call(functools.partial(kernel, ns, ntp), out_shape=jax.ShapeDty...]
where the time goes in v4:
time: 53.9 us; the launch traced here: 53.7 us
  Pallas kernels  51.8 us (96%)
  local copies, waits for them, and re-layouts  1.88 us (3%)
    pallas_call x1, Pallas kernels, per_device(): pl.pallas_call(functools.partial(kernel, ns, ntp), out_shape=jax.ShapeDty...  51.8 us
    unnamed x1, local copies, waits for them, and re-layouts  1.88 us

profile of v4, /device:TPU:5, one launch (start us, length us, event | category | flops | bytes accessed | tf_op | source)
XLA Modules:
  0.0 53.7 jit_solution(12389324338523857576)
XLA Ops:
  0.0 51.8 %shard_map.100 = bf16[128,2048]{1,0:T(8,128)(2,1)} custom-call(bf16[128,1024]{1,0:T(8,128)(2,1)} %tok_hbm.1, bf16[4096,2048]{1,0:T(8,128)(2,1)} %w_hbm.1, f32[4,2048]{1,0:T(4,128)} %cw_hbm.1, f32[1,2048]{1,0:T(1,128)} %bitcast.6, bf16[288,2048]{1,0:T(8,128)(2,1)} %bitcast.5, bf16[256,2048]{1,0:T(8,128)(2,1)} %dtw_hbm.1, f32[1,2048]{1,0:T(1,128)} %bitcast.7, ...), custom_call_target="tpu_custom_call" | custom-call | tf_op jit(solution)/shard_map/pallas_call | solution.py:511
  51.9 1.9 %copy.12 = bf16[128,2048]{1,0:T(8,128)(2,1)} copy(bf16[128,2048]{1,0:T(8,128)(2,1)} %shard_map.100) | data formatting | bytes 1048576

commit v5 on v4

--- a/solution.py
+++ b/solution.py
@@ -10,6 +10,7 @@
 MESH = pl.DeviceIdType.MESH
 LOG2E = 1.4426950408889634
 LANES = 128
+PIECES = 4
 
 
 def kernel(
@@ -82,8 +83,7 @@
     per = ag.shape[2]
     f32, bf16 = jnp.float32, jnp.bfloat16
     half = rows // 2
-    split = half - 16
-    token_rows = ((split, rows - split), (0, split))
+    piece = rows // PIECES
     phase_rows = (half, 0)
 
     small = [
@@ -130,7 +130,7 @@
     pl.semaphore_wait(barrier, ns + ntp - 2)
 
     def tok_copy(k, h, by, sems, own):
-        at = pl.ds(*token_rows[h])
+        at = pl.ds(h * piece, piece)
         return pltpu.make_async_remote_copy(
             src_ref=tok_hbm.at[at] if own else tok_all.at[k, at],
             dst_ref=tok_all.at[k, at],
@@ -167,27 +167,24 @@
                 tok_copy(z + d, h, -1, tok_left, False).start()
 
     tn = min(512, width)
-
-    def multiply(k, h, first):
-        if h == 0:
+    blocks = width // tn
+
+    def multiply(k, i, first):
+        if i == 0:
             w_copy(k).wait()
         part_k = pl.ds(pl.multiple_of(k * depth, depth), depth)
-        mine = pl.ds(*token_rows[h])
-
-        @pl.loop(0, width // tn)
-        def _(i):
-            at = pl.ds(pl.multiple_of(i * tn, tn), tn)
-            got = jnp.dot(tok_all[k, mine, :], w_ref[part_k, at], preferred_element_type=f32)
-            acc[mine, at] = got if first else acc[mine, at] + got
-
-    def multiply_pair(d, h):
+        at = pl.ds(i * tn, tn)
+        got = jnp.dot(tok_all[k], w_ref[part_k, at], preferred_element_type=f32)
+        acc[:, at] = got if first else acc[:, at] + got
+
+    def multiply_pair(d, i):
         @pl.when(z - d >= 0)
         def _():
-            multiply(z - d, h, False)
+            multiply(z - d, i, False)
 
         @pl.when(z + d < ntp)
         def _():
-            multiply(z + d, h, False)
+            multiply(z + d, i, False)
 
     halo = pltpu.make_async_remote_copy(
         src_ref=halo_out,
@@ -316,7 +313,7 @@
 
         zero = jnp.zeros((8, LANES), f32)
         states, total = lax.fori_loop(
-            r0, r0 + half, step, ([zero] * n_state, zero), unroll=8
+            r0, r0 + half, step, ([zero] * n_state, zero), unroll=16
         )
         if p == 0:
             for n in range(n_state):
@@ -371,7 +368,7 @@
             y3[at, :] = terms[0]
             return states
 
-        lax.fori_loop(0, rows, step, [entry[pl.ds(n * 8, 8), :] for n in range(n_state)], unroll=8)
+        lax.fori_loop(0, rows, step, [entry[pl.ds(n * 8, 8), :] for n in range(n_state)], unroll=16)
 
         @pl.loop(g * 8, jnp.minimum(g * 8 + 8, tiles))
         def _(j):
@@ -379,7 +376,8 @@
             y = y3[pl.ds(j, rows, stride=stride), :] + skip_ref[:, at] * u_ref[:, at].astype(f32)
             out_ref[:, at] = (y * sigmoid(4.0 * (y - thr_ref[:, at]))).astype(bf16)
 
-    send_own(0)
+    for h in range(PIECES):
+        send_own(h)
     in_copy(8).wait()
     in_copy(5).wait()
     for j in range(tiles):
@@ -387,40 +385,32 @@
         r3[pl.ds(j, n_state, stride=stride), :] = -LOG2E * jnp.exp(alog_ref[:, at])
     part[:, :, :, cols:] = jnp.zeros(part.shape[:3] + (part.shape[3] - cols,), f32)
     ps[:, :, :, cols:] = jnp.zeros(ps.shape[:3] + (ps.shape[3] - cols,), ps.dtype)
-    send_own(1)
-    multiply(z, 0, True)
-
-    @pl.loop(1, ntp)
+    for h in range(PIECES):
+        if ntp > 1:
+            take(1, h)
+        for i in range(h, blocks, PIECES):
+            multiply(z, i, True)
+
+    @pl.loop(2, ntp)
     def _(d):
-        take(d, 0)
-        multiply_pair(d, 0)
-
-        @pl.when(d < ntp - 1)
-        def _():
-            take(d, 1)
-
+        for h in range(PIECES):
+            take(d, h)
+            for i in range(h, blocks, PIECES):
+                multiply_pair(d - 1, i)
+
+    if ntp > 1:
+        for i in range(blocks):
+            multiply_pair(ntp - 1, i)
     halo_out[...] = acc[rows - 16 :, :].astype(bf16)
 
     @pl.when(q + 1 < ns)
     def _():
         halo.start()
 
-    pad[pl.ds(8 + split, rows - split), :] = acc[split:, :].astype(bf16).astype(f32)
+    pad[pl.ds(8, rows), :] = acc[...].astype(bf16).astype(f32)
     for i in (0, 1, 2):
         in_copy(i).wait()
     project(0)
-
-    multiply(z, 1, True)
-
-    @pl.loop(1, ntp - 1)
-    def _(d):
-        multiply_pair(d, 1)
-
-    reduce(0)
-    if ntp > 1:
-        take(ntp - 1, 1)
-        multiply_pair(ntp - 1, 1)
-    pad[pl.ds(8, split), :] = acc[:split, :].astype(bf16).astype(f32)
 
     @pl.when(q > 0)
     def _():
@@ -432,11 +422,12 @@
         pad[pl.ds(0, 8), :] = jnp.zeros((8, width), f32)
 
     project(1)
+    reduce(0)
+    reduce(1)
 
     in_copy(3).wait()
     in_copy(4).wait()
     prepare(0)
-    reduce(1)
 
     @pl.loop(0, groups)
     def _(g):
@@ -457,7 +448,7 @@
 
 
     for k in range(ntp):
-        for h in range(2):
+        for h in range(PIECES):
 
             @pl.when((z + 1 < ntp) & (k <= z))
             def _():
@@ -545,9 +536,9 @@
             pltpu.VMEM((n_state * 8, LANES), f32),
             dma((ntp,)),
             dma((9,)),
-            dma((ntp, 2)),
-            dma((ntp, 2)),
-            dma((ntp, 2)),
+            dma((ntp, PIECES)),
+            dma((ntp, PIECES)),
+            dma((ntp, PIECES)),
             dma((2,)),
             dma((2, ntp - 1)),
             dma((2, ntp - 1)),

time: 53.9 us -> 51.7 us (0.959)
  Pallas kernels: 51.8 us -> 49.7 us
    pallas_call x1, Pallas kernels: 51.8 us -> 49.7 us  [per_device(): pl.pallas_call(functools.partial(kernel, ns, ntp), out_shape=jax.ShapeDty...]
where the time goes in v5:
time: 51.7 us; the launch traced here: 51.6 us
  Pallas kernels  49.7 us (96%)
  local copies, waits for them, and re-layouts  1.88 us (4%)
    pallas_call x1, Pallas kernels, per_device(): pl.pallas_call(functools.partial(kernel, ns, ntp), out_shape=jax.ShapeDty...  49.7 us
    unnamed x1, local copies, waits for them, and re-layouts  1.88 us

profile of v5, /device:TPU:5, one launch (start us, length us, event | category | flops | bytes accessed | tf_op | source)
XLA Modules:
  0.0 51.6 jit_solution(10489911239098649697)
XLA Ops:
  0.0 49.7 %shard_map.100 = bf16[128,2048]{1,0:T(8,128)(2,1)} custom-call(bf16[128,1024]{1,0:T(8,128)(2,1)} %tok_hbm.1, bf16[4096,2048]{1,0:T(8,128)(2,1)} %w_hbm.1, f32[4,2048]{1,0:T(4,128)} %cw_hbm.1, f32[1,2048]{1,0:T(1,128)} %bitcast.6, bf16[288,2048]{1,0:T(8,128)(2,1)} %bitcast.5, bf16[256,2048]{1,0:T(8,128)(2,1)} %dtw_hbm.1, f32[1,2048]{1,0:T(1,128)} %bitcast.7, ...), custom_call_target="tpu_custom_call" | custom-call | tf_op jit(solution)/shard_map/pallas_call | solution.py:502
  49.7 1.9 %copy.12 = bf16[128,2048]{1,0:T(8,128)(2,1)} copy(bf16[128,2048]{1,0:T(8,128)(2,1)} %shard_map.100) | data formatting | bytes 1048576

commit v6 on v5

--- a/solution.py
+++ b/solution.py
@@ -10,7 +10,6 @@
 MESH = pl.DeviceIdType.MESH
 LOG2E = 1.4426950408889634
 LANES = 128
-PIECES = 4
 
 
 def kernel(
@@ -83,7 +82,7 @@
     per = ag.shape[2]
     f32, bf16 = jnp.float32, jnp.bfloat16
     half = rows // 2
-    piece = rows // PIECES
+    pieces, piece = tok_all.shape[1], tok_all.shape[3]
     phase_rows = (half, 0)
 
     small = [
@@ -95,8 +94,10 @@
         (alog_hbm, alog_ref),
         (skip_hbm, skip_ref),
         (thr_hbm, thr_ref),
-        (tok_hbm, tok_all.at[z]),
     ]
+    for h in range(tok_all.shape[1]):
+        part_h = pl.ds(h * tok_all.shape[3], tok_all.shape[3])
+        small.append((tok_hbm.at[:, part_h], tok_all.at[z, h]))
 
     def tile_at(j):
         return pl.ds(pl.multiple_of(j * LANES, LANES), LANES)
@@ -111,7 +112,8 @@
         part_k = pl.ds(pl.multiple_of(k * depth, depth), depth)
         return pltpu.make_async_copy(w_hbm.at[part_k], w_ref.at[part_k], w_sem.at[k])
 
-    in_copy(8).start()
+    for h in range(pieces):
+        in_copy(8 + h).start()
     w_copy(z).start()
 
     barrier = pltpu.get_barrier_semaphore()
@@ -132,8 +134,8 @@
     def tok_copy(k, h, by, sems, own):
         at = pl.ds(h * piece, piece)
         return pltpu.make_async_remote_copy(
-            src_ref=tok_hbm.at[at] if own else tok_all.at[k, at],
-            dst_ref=tok_all.at[k, at],
+            src_ref=tok_hbm.at[:, at] if own else tok_all.at[k, h],
+            dst_ref=tok_all.at[k, h],
             send_sem=sems.at[k, h],
             recv_sem=tok_recv.at[k, h],
             device_id={"tp": z + by},
@@ -169,22 +171,23 @@
     tn = min(512, width)
     blocks = width // tn
 
-    def multiply(k, i, first):
-        if i == 0:
+    def multiply(k, h, first):
+        if h == 0:
             w_copy(k).wait()
-        part_k = pl.ds(pl.multiple_of(k * depth, depth), depth)
-        at = pl.ds(i * tn, tn)
-        got = jnp.dot(tok_all[k], w_ref[part_k, at], preferred_element_type=f32)
-        acc[:, at] = got if first else acc[:, at] + got
-
-    def multiply_pair(d, i):
+        part_k = pl.ds(pl.multiple_of(k * depth + h * piece, piece), piece)
+        for i in range(blocks):
+            at = pl.ds(i * tn, tn)
+            got = jnp.dot(tok_all[k, h], w_ref[part_k, at], preferred_element_type=f32)
+            acc[:, at] = got if first else acc[:, at] + got
+
+    def multiply_pair(d, h):
         @pl.when(z - d >= 0)
         def _():
-            multiply(z - d, i, False)
+            multiply(z - d, h, False)
 
         @pl.when(z + d < ntp)
         def _():
-            multiply(z + d, i, False)
+            multiply(z + d, h, False)
 
     halo = pltpu.make_async_remote_copy(
         src_ref=halo_out,
@@ -376,31 +379,33 @@
             y = y3[pl.ds(j, rows, stride=stride), :] + skip_ref[:, at] * u_ref[:, at].astype(f32)
             out_ref[:, at] = (y * sigmoid(4.0 * (y - thr_ref[:, at]))).astype(bf16)
 
-    for h in range(PIECES):
+    for h in range(pieces):
         send_own(h)
-    in_copy(8).wait()
     in_copy(5).wait()
     for j in range(tiles):
         at = slice(j * LANES, (j + 1) * LANES)
         r3[pl.ds(j, n_state, stride=stride), :] = -LOG2E * jnp.exp(alog_ref[:, at])
     part[:, :, :, cols:] = jnp.zeros(part.shape[:3] + (part.shape[3] - cols,), f32)
     ps[:, :, :, cols:] = jnp.zeros(ps.shape[:3] + (ps.shape[3] - cols,), ps.dtype)
-    for h in range(PIECES):
+    for h in range(pieces):
+        in_copy(8 + h).wait()
+        multiply(z, h, h == 0)
+        if ntp > 2:
+            take(1, h)
+
+    @pl.loop(2, ntp - 1)
+    def _(d):
+        for h in range(pieces):
+            multiply_pair(d - 1, h)
+            take(d, h)
+
+    for h in range(pieces):
+        if ntp > 2:
+            multiply_pair(ntp - 2, h)
+    for h in range(pieces):
         if ntp > 1:
-            take(1, h)
-        for i in range(h, blocks, PIECES):
-            multiply(z, i, True)
-
-    @pl.loop(2, ntp)
-    def _(d):
-        for h in range(PIECES):
-            take(d, h)
-            for i in range(h, blocks, PIECES):
-                multiply_pair(d - 1, i)
-
-    if ntp > 1:
-        for i in range(blocks):
-            multiply_pair(ntp - 1, i)
+            take(ntp - 1, h)
+            multiply_pair(ntp - 1, h)
     halo_out[...] = acc[rows - 16 :, :].astype(bf16)
 
     @pl.when(q + 1 < ns)
@@ -448,7 +453,7 @@
 
 
     for k in range(ntp):
-        for h in range(PIECES):
+        for h in range(pieces):
 
             @pl.when((z + 1 < ntp) & (k <= z))
             def _():
@@ -495,6 +500,7 @@
     groups = stride // 8
     padded = -(-proj_weight.shape[1] // LANES) * LANES
     per = rows // 2 // ntp
+    pieces = max(1, depth // 256)
     f32, bf16 = jnp.float32, jnp.bfloat16
     sent = bf16 if per % 16 == 0 else f32
     dma = pltpu.SemaphoreType.DMA
@@ -514,7 +520,7 @@
             pltpu.VMEM(a_log.shape, f32),
             pltpu.VMEM((1, width), f32),
             pltpu.VMEM((1, width), f32),
-            pltpu.VMEM((ntp, rows, depth), bf16),
+            pltpu.VMEM((ntp, pieces, rows, depth // pieces), bf16),
             pltpu.VMEM((rows, width), f32),
             pltpu.VMEM((rows + 8, width), f32),
             pltpu.VMEM((16, width), bf16),
@@ -535,10 +541,10 @@
             pltpu.VMEM((groups, ns - 1, n_state * 8 + 16, LANES), bf16),
             pltpu.VMEM((n_state * 8, LANES), f32),
             dma((ntp,)),
-            dma((9,)),
-            dma((ntp, PIECES)),
-            dma((ntp, PIECES)),
-            dma((ntp, PIECES)),
+            dma((8 + pieces,)),
+            dma((ntp, pieces)),
+            dma((ntp, pieces)),
+            dma((ntp, pieces)),
             dma((2,)),
             dma((2, ntp - 1)),
             dma((2, ntp - 1)),

time: 51.7 us -> 50.5 us (0.977)
  Pallas kernels: 49.7 us -> 48.5 us
    pallas_call x1, Pallas kernels: 49.7 us -> 48.5 us  [per_device(): pl.pallas_call(functools.partial(kernel, ns, ntp), out_shape=jax.ShapeDty...]
where the time goes in v6:
time: 50.5 us; the launch traced here: 50.4 us
  Pallas kernels  48.5 us (96%)
  local copies, waits for them, and re-layouts  1.88 us (4%)
    pallas_call x1, Pallas kernels, per_device(): pl.pallas_call(functools.partial(kernel, ns, ntp), out_shape=jax.ShapeDty...  48.5 us
    unnamed x1, local copies, waits for them, and re-layouts  1.88 us

profile of v6, /device:TPU:5, one launch (start us, length us, event | category | flops | bytes accessed | tf_op | source)
XLA Modules:
  0.0 50.4 jit_solution(9472702290362069981)
XLA Ops:
  0.0 48.5 %shard_map.100 = bf16[128,2048]{1,0:T(8,128)(2,1)} custom-call(bf16[128,1024]{1,0:T(8,128)(2,1)} %tok_hbm.1, bf16[4096,2048]{1,0:T(8,128)(2,1)} %w_hbm.1, f32[4,2048]{1,0:T(4,128)} %cw_hbm.1, f32[1,2048]{1,0:T(1,128)} %bitcast.6, bf16[288,2048]{1,0:T(8,128)(2,1)} %bitcast.5, bf16[256,2048]{1,0:T(8,128)(2,1)} %dtw_hbm.1, f32[1,2048]{1,0:T(1,128)} %bitcast.7, ...), custom_call_target="tpu_custom_call" | custom-call | tf_op jit(solution)/shard_map/pallas_call | solution.py:508
  48.5 1.9 %copy.12 = bf16[128,2048]{1,0:T(8,128)(2,1)} copy(bf16[128,2048]{1,0:T(8,128)(2,1)} %shard_map.100) | data formatting | bytes 1048576
